TPU v7x, 512 devices: a whole 4x4x16 slice. The times are simulated.
512 devices in a mesh: seq: 64 (over z, y_lo, core), tp: 8 (over y_hi, x).
Axes of the slice: x: 4, y: 4 (y_hi: 2, y_lo: 2; y = y_hi * 2 + y_lo), z: 16, core: 2. Of those that a mesh axis runs over, the one named last changes fastest.
Arguments:
- queries: bfloat16 [8192, 1024], P('seq'), may hold values from -8 to 8
- key_rows: bfloat16 [8192, 256], P(('seq', 'tp')), may hold values from -4 to 4
- value_rows: bfloat16 [8192, 256], P(('seq', 'tp')), may hold values from -6 to 6
- ssm_input: bfloat16 [8192, 3072], P('seq', 'tp'), may hold values from -0.29882812 to 0.29882812
- gate_input: bfloat16 [8192, 3072], P('seq', 'tp'), may hold values from -6 to 6
- write_vectors: bfloat16 [8192, 256], P('seq'), may hold values from -1.5 to 1.5
- read_vectors: bfloat16 [8192, 256], P('seq'), may hold values from -1.5 to 1.5
- decay_rates: float32 [8192, 48], P('seq', 'tp'), may hold values from 0 to 3, as said below
- attn_out_weight: bfloat16 [1024, 2048], P('tp'), may hold values from -0.8984375 to 0.8984375
- ssm_out_weight: bfloat16 [3072, 2048], P('tp'), may hold values from -0.109375 to 0.109375
Outputs:
- mixer_output: float32 [8192, 2048], P(('seq', 'tp'))
Inputs may be any that keep to these rules, and one draw needn't show every extreme that they name: `decay_rates`: positive.
All inputs are finite; a program needn't handle non-finite values.
Results may differ from a plain program's by a relative error of at most 0.0045.
Values may be sent and summed in bfloat16 or wider, within the bound.
No kernel may reach another device: no remote copies, remote signals or barrier semaphores. Data moves between devices by JAX's collectives and lax.ppermute only.
A program may use at most 128 MiB of HBM per device.

v0:
```python
import math
import jax
import jax.numpy as jnp
from jax import lax
from jax.sharding import PartitionSpec as P

ASKER_PROBES = 8
KVHEADS = 2
HEAD = 128
precise = lax.Precision.HIGHEST
masked_score = -1e30


def prefix(value, axis, join, neutral):
    count, mine = (lax.axis_size(axis), lax.axis_index(axis))
    pieces = jax.tree.map(lambda part: lax.all_gather(part, axis), value)
    so_far = jax.tree.map(
        lambda part, zero: jnp.full_like(part, 0) + jnp.asarray(zero, part.dtype), value, neutral
    )

    def turn(position, so_far):
        longer = join(so_far, jax.tree.map(lambda part: part[position], pieces))
        return jax.tree.map(lambda new, old: jnp.where(position < mine, new, old), longer, so_far)

    return lax.fori_loop(0, count - 1, turn, so_far)


def combined_all(value, axis, join):
    pieces = jax.tree.map(lambda part: lax.all_gather(part, axis), value)
    head = jax.tree.map(lambda part: part[0], pieces)
    tail = jax.tree.map(lambda part: part[1:], pieces)
    so_far, _ = lax.scan(lambda so_far, slab: (join(so_far, slab), None), head, tail)
    return so_far


def local_states(ssm_input, write_vectors, read_vectors, decay_rates):
    local_rows = ssm_input.shape[0]
    heads_here = decay_rates.shape[1]
    values_f32 = ssm_input.astype(jnp.float32).reshape(local_rows, heads_here, -1)
    write_f32 = write_vectors.astype(jnp.float32)
    read_f32 = read_vectors.astype(jnp.float32)
    decay_sum = jnp.cumsum(-decay_rates, axis=0)
    block_decay = decay_sum[-1]
    positions = jnp.arange(local_rows)
    causal = (positions[:, None] >= positions[None, :])[:, :, None]
    decay_gap = jnp.where(causal, decay_sum[:, None, :] - decay_sum[None, :, :], 0.0)
    read_write = jnp.dot(read_vectors, write_vectors.T, preferred_element_type=jnp.float32)
    factor = jnp.where(causal, jnp.exp(decay_gap), 0.0) * read_write[:, :, None]
    within = jnp.einsum("tsh,shp->thp", factor, values_f32, precision=precise)
    block_state = jnp.einsum(
        "sh,shp,sn->hpn",
        jnp.exp(block_decay[None, :] - decay_sum),
        values_f32,
        write_f32,
        precision=precise,
    )
    return (within, block_state, decay_sum, read_f32)


def combine_states(earlier, later):
    return (earlier[0] * later[0], later[0][:, None, None] * earlier[1] + later[1])


def join_partial(first_part, second_part):
    updated_peak = jnp.maximum(first_part[0], second_part[0])
    first_scale = jnp.exp(first_part[0] - updated_peak)
    second_scale = jnp.exp(second_part[0] - updated_peak)
    running_sum = first_part[1] * first_scale + second_part[1] * second_scale
    weighted = first_part[2] * first_scale[..., None] + second_part[2] * second_scale[..., None]
    return (updated_peak, running_sum, weighted)


def local(
    queries,
    key_rows,
    value_rows,
    ssm_input,
    gate_input,
    write_vectors,
    read_vectors,
    decay_rates,
    attn_out_weight,
    ssm_out_weight,
):
    local_rows = queries.shape[0]
    within, block_state, decay_sum, read_f32 = local_states(
        ssm_input, write_vectors, read_vectors, decay_rates
    )
    block_decay = jnp.exp(decay_sum[-1])
    neutral = (jnp.ones_like(block_decay), jnp.zeros_like(block_state))
    entering = prefix((block_decay, block_state), "seq", combine_states, neutral)
    carried = jnp.einsum(
        "th,tn,hpn->thp", jnp.exp(decay_sum), read_f32, entering[1], precision=precise
    )
    ssm_raw = (within + carried).reshape(local_rows, -1)
    ssm_half = (ssm_raw * jax.nn.silu(gate_input.astype(jnp.float32))).astype(jnp.bfloat16)
    group = ASKER_PROBES // KVHEADS
    query_heads = queries.reshape(local_rows, KVHEADS, group, HEAD)
    slice_rows = key_rows.shape[0]
    seq_index = lax.axis_index("seq")
    tp_index = lax.axis_index("tp")
    query_place = seq_index * local_rows + jnp.arange(local_rows)
    score_scale = 1.0 / math.sqrt(HEAD)
    start_max = jnp.full((local_rows, KVHEADS, group), masked_score, jnp.float32)
    start_sum = jnp.zeros((local_rows, KVHEADS, group), jnp.float32)
    start_weighted = jnp.zeros((local_rows, KVHEADS, group, HEAD), jnp.float32)
    running = (start_max, start_sum, start_weighted)
    first_row = jnp.int32(0)
    key_segment = lax.all_gather(key_rows, "seq", axis=0, tiled=True)
    value_part = lax.all_gather(value_rows, "seq", axis=0, tiled=True)
    piece_rows = key_segment.shape[0]
    for lower_row in range(0, piece_rows, 256):
        upper_row = min(lower_row + 256, piece_rows)
        attend_key_segment = key_segment[lower_row:upper_row]
        attend_value_part = value_part[lower_row:upper_row]
        attend_first_row = first_row + lower_row
        attend_piece_rows = attend_key_segment.shape[0]
        row_ids = attend_first_row + jnp.arange(attend_piece_rows)
        key_place = (
            row_ids // slice_rows * local_rows + tp_index * slice_rows + row_ids % slice_rows
        )
        compute_running_max, compute_running_sum, compute_weighted = running
        key_block = attend_key_segment.reshape(attend_piece_rows, KVHEADS, HEAD)
        value_block = attend_value_part.reshape(attend_piece_rows, KVHEADS, HEAD)
        scores = (
            jnp.einsum("tgqd,ngd->tgqn", query_heads, key_block, preferred_element_type=jnp.float32)
            * score_scale
        )
        visible = (key_place[None, :] <= query_place[:, None])[:, None, None, :]
        scores = jnp.where(visible, scores, masked_score)
        updated_peak = jnp.maximum(compute_running_max, jnp.max(scores, axis=-1))
        weights = jnp.where(visible, jnp.exp(scores - updated_peak[..., None]), 0.0)
        factor = jnp.exp(compute_running_max - updated_peak)
        compute_running_sum = compute_running_sum * factor + jnp.sum(weights, axis=-1)
        compute_weighted = compute_weighted * factor[..., None] + jnp.einsum(
            "tgqn,ngd->tgqd",
            weights.astype(jnp.bfloat16),
            value_block,
            preferred_element_type=jnp.float32,
        )
        running = (updated_peak, compute_running_sum, compute_weighted)
    running_max, running_sum, weighted = running
    heads_mine = ASKER_PROBES // lax.axis_size("tp")
    running_max, running_sum, weighted = combined_all(
        (running_max, running_sum, weighted), "tp", join_partial
    )
    all_heads = (weighted / running_sum[..., None]).reshape(local_rows, ASKER_PROBES, HEAD)
    own_heads = lax.dynamic_slice_in_dim(all_heads, tp_index * heads_mine, heads_mine, 1)
    attn_half = own_heads.reshape(local_rows, heads_mine * HEAD).astype(jnp.bfloat16)
    attention_share = lax.psum_scatter(
        jnp.dot(attn_half, attn_out_weight, preferred_element_type=jnp.float32),
        "tp",
        scatter_dimension=0,
        tiled=True,
    )
    state_share = lax.psum_scatter(
        jnp.dot(ssm_half, ssm_out_weight, preferred_element_type=jnp.float32),
        "tp",
        scatter_dimension=0,
        tiled=True,
    )
    summed = attention_share + state_share
    return summed


def solution(mesh):
    placed = (
        P("seq", None),
        P(("seq", "tp"), None),
        P(("seq", "tp"), None),
        P("seq", "tp"),
        P("seq", "tp"),
        P("seq", None),
        P("seq", None),
        P("seq", "tp"),
        P("tp", None),
        P("tp", None),
    )
    return jax.shard_map(
        local, mesh=mesh, in_specs=placed, out_specs=P(("seq", "tp"), None), check_vma=False
    )
```

profile of v0, /device:TPU:2, one launch (start us, length us, event | category | flops | bytes accessed | tf_op | source)
XLA Modules:
  0.0 597.1 jit_solution(9801647952218511953)
XLA Ops:
  6.6 1.2 reshape.438
  7.8 71.4 %all_gather.30 = bf16[1024,256]{1,0:T(8,128)(2,1)S(1)} all-gather(bf16[16,256]{1,0:T(8,128)(2,1)} %param.15), channel_id=1, replica_groups=mesh['seq'=64,'tp'=8] {'seq'}, dimensions={0}, use_global_device_ids=true | all-gather | bytes 532480 | tf_op jit(solution)/shard_map/all_gather | solution.py:109
  80.3 61.2 %all_gather.33 = bf16[1024,256]{1,0:T(8,128)(2,1)S(1)} all-gather(bf16[16,256]{1,0:T(8,128)(2,1)} %param.16), channel_id=1, replica_groups=mesh['seq'=64,'tp'=8] {'seq'}, dimensions={0}, use_global_device_ids=true | all-gather | bytes 532480 | tf_op jit(solution)/shard_map/all_gather | solution.py:110
  144.2 1.3 fusion.106
  148.0 1.7 fusion.19
  152.8 1.4 fusion.23
  154.2 1.4 fusion.25
  155.6 1.4 fusion.27
  158.0 34.1 %all_gather.32 = f32[8,128,2,4]{1,3,2,0:T(4,128)S(1)} all-gather(f32[1,128,2,4]{1,3,2,0:T(4,128)S(1)} %get-tuple-element.225), channel_id=1, replica_groups=mesh['seq'=64,'tp'=8] {'tp'}, dimensions={0}, use_global_device_ids=true | all-gather | bytes 36864 | tf_op jit(solution)/shard_map/all_gather | solution.py:29
  192.0 34.1 %all_gather.31 = f32[8,128,2,4]{1,3,2,0:T(4,128)S(1)} all-gather(f32[1,128,2,4]{1,3,2,0:T(4,128)S(1)} %get-tuple-element.226), channel_id=1, replica_groups=mesh['seq'=64,'tp'=8] {'tp'}, dimensions={0}, use_global_device_ids=true | all-gather | bytes 36864 | tf_op jit(solution)/shard_map/all_gather | solution.py:29
  226.2 62.5 %all-gather.2 = f32[64,1,6]{2,1,0:T(1,128)} all-gather(f32[1,1,6]{2,1,0:T(1,128)S(1)} %copy-done.21), channel_id=1, replica_groups=mesh['seq'=64,'tp'=8] {'seq'}, dimensions={0}, use_global_device_ids=true | all-gather | bytes 1560 | tf_op jit(solution)/shard_map/all_gather | solution.py:16
  288.9 1.3 convolution_bitcast_fusion.5
  291.7 4.2 slice.76
  295.8 18.7 %while.28 = (s32[]{:T(128)}, f32[128,2,4]{0,2,1:T(4,128)S(1)}, f32[128,2,4]{0,2,1:T(4,128)S(1)}, f32[128,2,4,128]{3,2,1,0:T(4,128)S(1)}, f32[7,128,2,4]{1,3,2,0:...) while((s32[]{:T(128)}, f32[128,2,4]{0,2,1:T(4,128)S(1)}, ...), condition=%wide.region_9.10_spmd, body=%wide.region_8.9_spmd.sunk | while | flops 399362 | bytes 2678885 | solution.py:32
  297.3 1.2 fusion.126
  299.9 1.2 fusion.126
  302.6 1.2 fusion.126
  305.3 1.2 fusion.126
  310.6 1.2 fusion.126
  313.3 1.2 fusion.126
  315.4 72.6 %all-gather.8.cloned.1.call-done = f32[384,64,256]{2,1,0:T(8,128)} async-done(((f32[6,64,256]{2,1,0:T(8,128)}), f32[384,64,256]{2,1,0:T(8,128)}) %all-gather.8.cloned.1.call-update) | async-done | bytes 25165840 | tf_op jit(solution)/shard_map/all_gather | solution.py:16
  388.0 114.7 %while.29 = (s32[]{:T(128)}, f32[6,64,256]{2,1,0:T(8,128)S(1)}, s32[]{:T(128)}, f32[64,6]{1,0:T(8,128)}, f32[64,6,64,256]{3,2,1,0:T(8,128)}, /*index=5*/s32[]{:T(128)}, s32[]{:T(128)}) while((s32[]{:T(128)}, f32[6,64,256]{2,1,0:T(8,128)S(1)}, s32[]{:T(128)}, f32[64,6]{1,0:T(8,128)}, f32[64,6,64,256]{3,2,1,0:T(8,128)}, ...), condition=%wide.region_13.14_spmd.clone, body=%wide.region_12.13_spmd.clone.sunk | while | flops 393220 | bytes 1179833 | solution.py:25
  503.2 2.3 convolution_add_fusion
  505.6 85.0 %reduce-scatter.2.cloned.1.call-done = f32[16,2048]{1,0:T(8,128)} async-done(((f32[128,2048]{1,0:T(8,128)}), f32[16,2048]{1,0:T(8,128)}) %reduce-scatter.2.cloned.1.call-update) | async-done | bytes 131088 | tf_op jit(solution)/shard_map/reduce_scatter | solution.py:150
  (256 shorter events, 137.2 us)
Async XLA Ops:
  6.5 496.7 %copy-start = (bf16[384,2048]{1,0:T(8,128)(2,1)S(1)}, bf16[384,2048]{1,0:T(8,128)(2,1)}, u32[]{:S(2)}) copy-start(bf16[384,2048]{1,0:T(8,128)(2,1)} %param.23) | copy-start | bytes 4718596
  6.5 283.7 %all-gather.6.cloned.1.call-start = ((), (), s32[]{:S(2)}) async-start(), calls=%async_computation.1 | async-start | bytes 4718592 | tf_op jit(solution)/shard_map/all_gather | solution.py:29
  143.9 2.8 copy-start.7
  144.2 3.0 copy-start.6
  145.5 2.1 copy-start.13
  145.5 2.1 copy-start.5
  145.9 2.1 copy-start.1
  146.3 1.7 copy-start.2
  146.3 1.7 copy-start.15
  146.7 1.3 copy-start.3
  146.7 1.3 copy-start.17
  147.1 2.6 copy-start.20
  147.1 3.5 copy-start.12
  147.1 3.7 copy-start.8
  149.7 139.0 %copy-start.9 = (bf16[128,256]{1,0:T(8,128)(2,1)S(1)}, bf16[128,256]{1,0:T(8,128)(2,1)}, u32[]{:S(2)}) copy-start(bf16[128,256]{1,0:T(8,128)(2,1)} %param.20) | copy-start | bytes 196612
  149.7 238.3 %all-gather.8.cloned.1.call-start = ((), (), s32[]{:S(2)}) async-start(), calls=%async_computation.2 | async-start | bytes 25559040 | tf_op jit(solution)/shard_map/all_gather | solution.py:16
  150.8 6.4 %copy-start.16 = (f32[128,2,4]{0,2,1:T(4,128)S(1)}, f32[128,2,4]{0,2,1:T(4,128)}, u32[]{:S(2)}) copy-start(f32[128,2,4]{0,2,1:T(4,128)} %copy-done.15) | copy-start | bytes 12292
  150.8 6.4 %copy-start.18 = (f32[128,2,4]{0,2,1:T(4,128)S(1)}, f32[128,2,4]{0,2,1:T(4,128)}, u32[]{:S(2)}) copy-start(f32[128,2,4]{0,2,1:T(4,128)} %copy-done.17) | copy-start | bytes 12292
  150.9 75.3 %copy-start.21 = (f32[1,1,6]{2,1,0:T(1,128)S(1)}, f32[1,1,6]{2,1,0:T(1,128)}, u32[]{:S(2)}) copy-start(f32[1,1,6]{2,1,0:T(1,128)} %get-tuple-element.224) | copy-start | bytes 76
  152.0 438.6 %reduce-scatter.2.cloned.1.call-start = ((), (), s32[]{:S(2)}) async-start(), calls=%async_computation.3 | async-start | bytes 1179648 | tf_op jit(solution)/shard_map/reduce_scatter | solution.py:150
  295.8 19.2 %copy-start.4 = (bf16[128,2048]{1,0:T(8,128)(2,1)S(1)}, bf16[128,2048]{1,0:T(8,128)(2,1)}, u32[]{:S(2)}) copy-start(bf16[128,2048]{1,0:T(8,128)(2,1)} %param.22) | copy-start | bytes 1572868
  315.1 187.6 %copy-start.19 = (f32[128,6]{0,1:T(8,128)S(1)}, f32[128,6]{0,1:T(8,128)}, u32[]{:S(2)}) copy-start(f32[128,6]{0,1:T(8,128)} %copy.97) | copy-start | bytes 9220
  315.4 187.4 %copy-start.10 = (bf16[128,256]{1,0:T(8,128)(2,1)S(1)}, bf16[128,256]{1,0:T(8,128)(2,1)}, u32[]{:S(2)}) copy-start(bf16[128,256]{1,0:T(8,128)(2,1)} %param.20) | copy-start | bytes 196612
  315.4 187.4 %copy-start.11 = (f32[128,6,64]{0,2,1:T(8,128)S(1)}, f32[128,6,64]{0,2,1:T(8,128)}, u32[]{:S(2)}) copy-start(f32[128,6,64]{0,2,1:T(8,128)} %convolution_bitcast_fusion.5) | copy-start | bytes 589828
  (1 other events, 1.2 us)
Sparse Core Ops, SparseCore 0:
  149.8 81.3 all-gather.5
  233.4 154.5 all-gather.7
  505.7 84.7 reduce-scatter.1
where the time goes:
time: 602 us; the launch traced here: 597 us
  blocking collectives  263 us (44%)
  waiting for transfers between devices  158 us (26%)
  other arithmetic  84.3 us (14%)
  local copies, waits for them, and re-layouts  65.5 us (11%)
  between operations  13.6 us (2%)
  matrix products  10.7 us (2%)
    reduce_scatter x1, waiting for transfers between devices, local(): lax.psum_scatter(jnp.dot(attn_half, attn_out_weight, preferred_element_ty...  85 us
    all_gather x1, waiting for transfers between devices, prefix(): pieces = jax.tree.map(lambda part: lax.all_gather(part, axis), value)  72.6 us
    all_gather x1, blocking collectives, local(): key_segment = lax.all_gather(key_rows, 'seq', axis=0, tiled=True)  71.4 us
    select_n x63, other arithmetic, turn(): jnp.where(position < mine, new, old)  69.8 us
    all_gather x2, blocking collectives, combined_all(): pieces = jax.tree.map(lambda part: lax.all_gather(part, axis), value)  68.2 us
    all_gather x1, blocking collectives, prefix(): pieces = jax.tree.map(lambda part: lax.all_gather(part, axis), value)  62.5 us
    all_gather x1, blocking collectives, local(): value_part = lax.all_gather(value_rows, 'seq', axis=0, tiled=True)  61.2 us
    mul x63, local copies, waits for them, and re-layouts, combine_states(): later[0][:, None, None] * earlier[1] + later[1]  43.3 us
  transfers between devices with their start and end apart: 3, of which 2 were waited for; matrix products, arithmetic and copies ran while one was open for 6% of the time, Pallas kernels for 0%

commit v1 on v0

--- a/solution.py
+++ b/solution.py
@@ -107,7 +107,9 @@
     running = (start_max, start_sum, start_weighted)
     first_row = jnp.int32(0)
     key_segment = lax.all_gather(key_rows, "seq", axis=0, tiled=True)
-    value_part = lax.all_gather(value_rows, "seq", axis=0, tiled=True)
+    value_part = jnp.concatenate(
+        lax.all_to_all(jnp.stack([value_rows] * lax.axis_size("seq")), "seq", 0, 0), axis=0
+    )
     piece_rows = key_segment.shape[0]
     for lower_row in range(0, piece_rows, 256):
         upper_row = min(lower_row + 256, piece_rows)

time: 602 us -> 588 us (0.977)
  blocking collectives: 263 us -> 211 us
  starting transfers between devices: 0.09 us -> 17.2 us
  matrix products: 10.7 us -> 17.6 us
    all_gather x1 -> x0, blocking collectives: 61.2 us -> none  [local(): value_part = lax.all_gather(value_rows, 'seq', axis=0, tiled=True)]
    all_to_all x0 -> x1, starting transfers between devices: none -> 17.1 us  [local(): lax.all_to_all(jnp.stack([value_rows] * lax.axis_size('seq')), 'seq', 0, 0)]
    all_gather x1, blocking collectives: 71.4 us -> 80.1 us  [local(): key_segment = lax.all_gather(key_rows, 'seq', axis=0, tiled=True)]
  transfers between devices with their start and end apart: 3 -> 4, of which waited for: 2 -> 2; matrix products, arithmetic and copies ran while one was open for 6% -> 9% of each run, Pallas kernels for 0% -> 0%
where the time goes in v1:
time: 588 us; the launch traced here: 582 us
  blocking collectives  211 us (36%)
  waiting for transfers between devices  160 us (27%)
  other arithmetic  89.2 us (15%)
  local copies, waits for them, and re-layouts  71.2 us (12%)
  matrix products  17.6 us (3%)
  starting transfers between devices  17.2 us (3%)
  between operations  13.5 us (2%)
    reduce_scatter x1, waiting for transfers between devices, local(): lax.psum_scatter(jnp.dot(attn_half, attn_out_weight, preferred_element_ty...  84.8 us
    all_gather x1, blocking collectives, local(): key_segment = lax.all_gather(key_rows, 'seq', axis=0, tiled=True)  80.1 us
    all_gather x1, waiting for transfers between devices, prefix(): pieces = jax.tree.map(lambda part: lax.all_gather(part, axis), value)  75.5 us
    select_n x63, other arithmetic, turn(): jnp.where(position < mine, new, old)  69.8 us
    all_gather x2, blocking collectives, combined_all(): pieces = jax.tree.map(lambda part: lax.all_gather(part, axis), value)  68.2 us
    all_gather x1, blocking collectives, prefix(): pieces = jax.tree.map(lambda part: lax.all_gather(part, axis), value)  62.9 us
    mul x63, local copies, waits for them, and re-layouts, combine_states(): later[0][:, None, None] * earlier[1] + later[1]  43.1 us
    all_to_all x1, starting transfers between devices, local(): lax.all_to_all(jnp.stack([value_rows] * lax.axis_size('seq')), 'seq', 0, 0)  17.1 us
  transfers between devices with their start and end apart: 4, of which 2 were waited for; matrix products, arithmetic and copies ran while one was open for 9% of the time, Pallas kernels for 0%

profile of v1, /device:TPU:2, one launch (start us, length us, event | category | flops | bytes accessed | tf_op | source)
XLA Modules:
  0.0 582.2 jit_solution(8685245784564562498)
XLA Ops:
  6.5 1.7 stack.2
  8.2 17.1 %all-to-all-start = ((bf16[64,16,256]{2,1,0:T(8,128)(2,1)}), bf16[64,16,256]{2,1,0:T(8,128)(2,1)S(1)}, u32[]{:S(2)}, u32[]{:S(2)}) async-start(bf16[64,16,256]{2,1,0:T(8,128)(2,1)} %stack.2), calls=%async_computation | async-start | bytes 1048576 | tf_op jit(solution)/shard_map/all_to_all | solution.py:111
  25.4 80.1 %all_gather.27 = bf16[1024,256]{1,0:T(8,128)(2,1)S(1)} all-gather(bf16[16,256]{1,0:T(8,128)(2,1)} %param.15), channel_id=1, replica_groups=mesh['seq'=64,'tp'=8] {'seq'}, dimensions={0}, use_global_device_ids=true | all-gather | bytes 532480 | tf_op jit(solution)/shard_map/all_gather | solution.py:109
  109.9 1.3 fusion.108
  111.2 2.3 fusion.107
  114.1 2.2 fusion.109
  116.9 1.3 fusion.110
  123.5 1.8 convolution_bitcast_fusion.1
  125.8 2.4 fusion.19
  130.7 1.5 fusion.23
  132.4 1.4 fusion.27
  134.1 34.1 %all_gather.29 = f32[8,128,2,4]{1,3,2,0:T(4,128)S(1)} all-gather(f32[1,128,2,4]{1,3,2,0:T(4,128)S(1)} %get-tuple-element.225), channel_id=1, replica_groups=mesh['seq'=64,'tp'=8] {'tp'}, dimensions={0}, use_global_device_ids=true | all-gather | bytes 36864 | tf_op jit(solution)/shard_map/all_gather | solution.py:29
  168.8 34.1 %all_gather.28 = f32[8,128,2,4]{1,3,2,0:T(4,128)S(1)} all-gather(f32[1,128,2,4]{1,3,2,0:T(4,128)S(1)} %get-tuple-element.226), channel_id=1, replica_groups=mesh['seq'=64,'tp'=8] {'tp'}, dimensions={0}, use_global_device_ids=true | all-gather | bytes 36864 | tf_op jit(solution)/shard_map/all_gather | solution.py:29
  203.5 62.9 %all-gather.2 = f32[64,1,6]{2,1,0:T(1,128)} all-gather(f32[1,1,6]{2,1,0:T(1,128)S(1)} %get-tuple-element.224), channel_id=1, replica_groups=mesh['seq'=64,'tp'=8] {'seq'}, dimensions={0}, use_global_device_ids=true | all-gather | bytes 1560 | tf_op jit(solution)/shard_map/all_gather | solution.py:16
  266.6 1.3 convolution_bitcast_fusion.5
  269.4 4.1 slice.80
  273.5 23.5 %while.28 = (s32[]{:T(128)}, f32[128,2,4]{0,2,1:T(4,128)S(1)}, f32[128,2,4]{0,2,1:T(4,128)S(1)}, f32[128,2,4,128]{3,2,1,0:T(4,128)S(1)}, f32[7,128,2,4]{1,3,2,0:...) while((s32[]{:T(128)}, f32[128,2,4]{0,2,1:T(4,128)S(1)}, ...), condition=%wide.region_9.10_spmd, body=%wide.region_8.9_spmd.sunk | while | flops 399362 | bytes 2678885 | solution.py:32
  279.1 1.2 fusion.126
  289.1 1.2 fusion.126
  295.8 1.2 fusion.126
  297.9 75.5 %all-gather.8.cloned.1.call-done = f32[384,64,256]{2,1,0:T(8,128)} async-done(((f32[6,64,256]{2,1,0:T(8,128)}), f32[384,64,256]{2,1,0:T(8,128)}) %all-gather.8.cloned.1.call-update) | async-done | bytes 25165840 | tf_op jit(solution)/shard_map/all_gather | solution.py:16
  373.4 114.6 %while.29 = (s32[]{:T(128)}, f32[6,64,256]{2,1,0:T(8,128)S(1)}, s32[]{:T(128)}, f32[64,6]{1,0:T(8,128)}, f32[64,6,64,256]{3,2,1,0:T(8,128)}, /*index=5*/s32[]{:T(128)}, s32[]{:T(128)}) while((s32[]{:T(128)}, f32[6,64,256]{2,1,0:T(8,128)S(1)}, s32[]{:T(128)}, f32[64,6]{1,0:T(8,128)}, f32[64,6,64,256]{3,2,1,0:T(8,128)}, ...), condition=%wide.region_13.14_spmd.clone, body=%wide.region_12.13_spmd.clone.sunk | while | flops 393220 | bytes 1179833 | solution.py:25
  488.5 2.4 convolution_add_fusion
  490.8 84.8 %reduce-scatter.2.cloned.1.call-done = f32[16,2048]{1,0:T(8,128)} async-done(((f32[128,2048]{1,0:T(8,128)}), f32[16,2048]{1,0:T(8,128)}) %reduce-scatter.2.cloned.1.call-update) | async-done | bytes 131088 | tf_op jit(solution)/shard_map/reduce_scatter | solution.py:152
  (258 shorter events, 150.9 us)
Async XLA Ops:
  6.5 481.9 %copy-start = (bf16[384,2048]{1,0:T(8,128)(2,1)S(1)}, bf16[384,2048]{1,0:T(8,128)(2,1)}, u32[]{:S(2)}) copy-start(bf16[384,2048]{1,0:T(8,128)(2,1)} %param.23) | copy-start | bytes 4718596
  8.2 111.2 %all-to-all-start = ((bf16[64,16,256]{2,1,0:T(8,128)(2,1)}), bf16[64,16,256]{2,1,0:T(8,128)(2,1)S(1)}, u32[]{:S(2)}, u32[]{:S(2)}) async-start(bf16[64,16,256]{2,1,0:T(8,128)(2,1)} %stack.2), calls=%async_computation | async-start | bytes 1048576 | tf_op jit(solution)/shard_map/all_to_all | solution.py:111
  25.3 242.6 %all-gather.6.cloned.1.call-start = ((), (), s32[]{:S(2)}) async-start(), calls=%async_computation.2 | async-start | bytes 4718592 | tf_op jit(solution)/shard_map/all_gather | solution.py:29
  109.7 7.3 %copy-start.4 = (bf16[256,256]{0,1:T(8,128)(2,1)S(1)}, bf16[256,256]{0,1:T(8,128)(2,1)}, u32[]{:S(2)}) copy-start(bf16[256,256]{0,1:T(8,128)(2,1)} %copy.127) | copy-start | bytes 393220
  111.1 5.2 copy-start.11
  113.4 4.8 copy-start.13
  120.2 5.6 copy-start.20
  123.1 2.3 copy-start.2
  123.1 2.7 copy-start.1
  123.5 4.8 copy-start.21
  123.5 5.3 copy-start.6
  125.3 3.3 copy-start.10
  128.2 5.9 %copy-start.12 = (f32[128,2,4]{0,2,1:T(4,128)S(1)}, f32[128,2,4]{0,2,1:T(4,128)}, u32[]{:S(2)}) copy-start(f32[128,2,4]{0,2,1:T(4,128)} %copy-done.11) | copy-start | bytes 12292
  128.2 5.9 %copy-start.14 = (f32[128,2,4]{0,2,1:T(4,128)S(1)}, f32[128,2,4]{0,2,1:T(4,128)}, u32[]{:S(2)}) copy-start(f32[128,2,4]{0,2,1:T(4,128)} %copy-done.13) | copy-start | bytes 12292
  128.2 5.9 %copy-start.16 = (f32[128,2,4]{0,2,1:T(4,128)S(1)}, f32[128,2,4]{0,2,1:T(4,128)}, u32[]{:S(2)}) copy-start(f32[128,2,4]{0,2,1:T(4,128)} %copy-done.15) | copy-start | bytes 12292
  128.2 5.9 %copy-start.18 = (f32[128,2,4]{0,2,1:T(4,128)S(1)}, f32[128,2,4]{0,2,1:T(4,128)}, u32[]{:S(2)}) copy-start(f32[128,2,4]{0,2,1:T(4,128)} %copy-done.17) | copy-start | bytes 12292
  128.2 138.3 %copy-start.7 = (bf16[128,256]{1,0:T(8,128)(2,1)S(1)}, bf16[128,256]{1,0:T(8,128)(2,1)}, u32[]{:S(2)}) copy-start(bf16[128,256]{1,0:T(8,128)(2,1)} %param.20) | copy-start | bytes 196612
  128.2 245.2 %all-gather.8.cloned.1.call-start = ((), (), s32[]{:S(2)}) async-start(), calls=%async_computation.3 | async-start | bytes 25559040 | tf_op jit(solution)/shard_map/all_gather | solution.py:16
  129.9 445.8 %reduce-scatter.2.cloned.1.call-start = ((), (), s32[]{:S(2)}) async-start(), calls=%async_computation.4 | async-start | bytes 1179648 | tf_op jit(solution)/shard_map/reduce_scatter | solution.py:152
  130.7 3.1 copy-start.3
  273.5 24.1 %copy-start.5 = (bf16[128,2048]{1,0:T(8,128)(2,1)S(1)}, bf16[128,2048]{1,0:T(8,128)(2,1)}, u32[]{:S(2)}) copy-start(bf16[128,2048]{1,0:T(8,128)(2,1)} %param.22) | copy-start | bytes 1572868
  297.6 190.4 %copy-start.19 = (f32[128,6]{0,1:T(8,128)S(1)}, f32[128,6]{0,1:T(8,128)}, u32[]{:S(2)}) copy-start(f32[128,6]{0,1:T(8,128)} %copy.92) | copy-start | bytes 9220
  297.9 190.1 %copy-start.8 = (bf16[128,256]{1,0:T(8,128)(2,1)S(1)}, bf16[128,256]{1,0:T(8,128)(2,1)}, u32[]{:S(2)}) copy-start(bf16[128,256]{1,0:T(8,128)(2,1)} %param.20) | copy-start | bytes 196612
  297.9 190.1 %copy-start.9 = (f32[128,6,64]{0,2,1:T(8,128)S(1)}, f32[128,6,64]{0,2,1:T(8,128)}, u32[]{:S(2)}) copy-start(f32[128,6,64]{0,2,1:T(8,128)} %convolution_bitcast_fusion.5) | copy-start | bytes 589828
  (2 other events, 2.5 us)
Sparse Core Ops, SparseCore 0:
  128.3 88.1 all-gather.5
  218.7 154.6 all-gather.7
  491.0 84.6 reduce-scatter.1
